TPU v7x, 128 devices: a whole 4x4x4 slice. The times are simulated.
128 devices in a mesh: row: 4 (over x_hi, core), reader: 32 (over x_lo, z, y).
Axes of the slice: x: 4 (x_hi: 2, x_lo: 2; x = x_hi * 2 + x_lo), y: 4, z: 4, core: 2. Of those that a mesh axis runs over, the one named last changes fastest.
Arguments:
- records: bfloat16 [4, 32, 256, 4096], P('row', None, 'reader'), may hold values from -6 to 6
- lengths: int32 [4, 32], replicated, may hold values from 1 to 256, as said below
- assignment: int32 [4, 32], replicated, may hold values from 0 to 31, as said below
- segment_ids: int32 [4, 32, 256], replicated, may hold values from 0 to 11, never falling along the last dimension, each value on 1 to 64 neighbouring positions
- norm_gain: float32 [4096], replicated, may hold values from 0.6 to 6
- w_qkv: bfloat16 [4096, 4, 1280], P('reader', 'row'), may hold values from -0.09375 to 0.09375
- w_out: bfloat16 [4096, 4, 1024], P('reader', 'row'), may hold values from -0.09375 to 0.09375
- score_weights: float32 [4096], replicated, may hold values from -0.09375 to 0.09375
Outputs:
- hidden_out: bfloat16 [28672, 4096], P('reader', 'row')
- record_scores: float32 [32, 4], P('reader')
Inputs may be any that keep to these rules, and one draw needn't show every extreme that they name: `assignment`: each row names every scorer shard exactly once. For every scorer shard the lengths of the records that name it, one from each row, sum to 896; some record has 256. `segment_ids`: along a record the document numbers never fall.
All inputs are finite; a program needn't handle non-finite values.
Results may differ from a plain program's by a relative error of at most 0.015.
The roundings to bfloat16 on the way count: a program that leaves them out, or rounds other values in their place, can miss the bound.
Values may be sent and summed in bfloat16 or wider, within the bound.
No kernel may reach another device: no remote copies, remote signals or barrier semaphores. Data moves between devices by JAX's collectives and lax.ppermute only.
A program may use at most 128 MiB of HBM per device.

v0:
```python
import math
import jax
import jax.numpy as jnp
from jax import lax
from jax.sharding import PartitionSpec as P

HS = 128
GROUP = 8
RECLEN = 256
ROPE_BASE = 500000.0


def rotary(values, cosine, sine):
    half = values.shape[-1] // 2
    shape = (values.shape[0],) + (1,) * (values.ndim - 2) + (half,)
    cosine = cosine.reshape(shape)
    sine = sine.reshape(shape)
    first = values[..., :half]
    second = values[..., half:]
    return jnp.concatenate(
        [first * cosine - second * sine, second * cosine + first * sine], axis=-1
    )


def masked_softmax(logits, allowed):
    held = jnp.where(allowed, logits, -1e30)
    top = jnp.max(held, axis=-1, keepdims=True)
    weights = jnp.where(allowed, jnp.exp(held - top), 0.0)
    return weights / jnp.sum(weights, axis=-1, keepdims=True)


def on_device(records, lengths, assignment, segment_ids, norm_gain, w_qkv, w_out, score_weights):
    row_count = lax.axis_size("row")
    reader_count = lax.axis_size("reader")
    row_index = lax.axis_index("row")
    reader_index = lax.axis_index("reader")
    slot_count = records.shape[2]
    width = records.shape[3]
    local_heads = w_qkv.shape[1]
    tok_rows = row_count * RECLEN - RECLEN // 2
    row_ids = jnp.arange(row_count, dtype=jnp.int32)
    chosen = jnp.argmax(assignment == reader_index, axis=1)
    record_lens = jnp.take_along_axis(lengths, chosen[:, None], axis=1)[:, 0]
    ends = jnp.cumsum(record_lens)
    starts = ends - record_lens
    place = jnp.arange(tok_rows, dtype=jnp.int32)
    owner = jnp.sum((place[:, None] >= ends[None, :-1]).astype(jnp.int32), axis=1)
    matches = owner[:, None] == row_ids[None, :]
    within = place - jnp.sum(jnp.where(matches, starts[None, :], 0), axis=1)
    picked = jnp.sum(jnp.where(matches, chosen[None, :], 0), axis=1)
    segs = segment_ids[owner, picked, within]
    own_assign = lax.dynamic_index_in_dim(assignment, row_index, 0, keepdims=False)
    readers = jnp.arange(reader_count, dtype=jnp.int32)
    outgoing = jnp.argmax(own_assign[None, :] == readers[:, None], axis=1)
    send_block = records[0][outgoing]
    arrived = lax.all_to_all(send_block, "reader", split_axis=0, concat_axis=0, tiled=True)
    own_record = arrived.reshape(1, reader_count * slot_count, width)
    gathered = lax.all_gather(own_record, "row", axis=0, tiled=True)
    packed = gathered.reshape(row_count * RECLEN, width)[owner * RECLEN + within]
    packed_f = packed.astype(jnp.float32)
    scale = lax.rsqrt(jnp.mean(packed_f * packed_f, axis=1, keepdims=True) + 1e-05)
    normed = (packed_f * scale * norm_gain).astype(jnp.bfloat16)
    full_qkv, full_out = (
        lax.all_gather(w_qkv, "reader", axis=0, tiled=True),
        lax.all_gather(w_out, "reader", axis=0, tiled=True),
    )
    projected = jnp.dot(normed, full_qkv.reshape(width, -1), preferred_element_type=jnp.float32)
    projected = projected.reshape(tok_rows, local_heads, GROUP + 2, HS)
    inv_freq = ROPE_BASE ** (-(jnp.arange(HS // 2, dtype=jnp.float32) * 2.0 / HS))
    angle = within.astype(jnp.float32)[:, None] * inv_freq[None, :]
    cosine = jnp.cos(angle)
    sine = jnp.sin(angle)
    queries = rotary(projected[:, :, :GROUP], cosine, sine).astype(jnp.bfloat16)
    keys = rotary(projected[:, :, GROUP], cosine, sine).astype(jnp.bfloat16)
    values = projected[:, :, GROUP + 1].astype(jnp.bfloat16)
    allowed = (
        (owner[:, None] == owner[None, :])
        & (segs[:, None] == segs[None, :])
        & (place[None, :] <= place[:, None])
    )
    logits = jnp.einsum("qhgd,khd->hgqk", queries, keys, preferred_element_type=jnp.float32) * (
        1.0 / math.sqrt(HS)
    )
    probs = masked_softmax(logits, allowed[None, None]).astype(jnp.bfloat16)
    mixed = jnp.einsum("hgqk,khd->qhgd", probs, values, preferred_element_type=jnp.float32).astype(
        jnp.bfloat16
    )
    mixed_flat = mixed.reshape(tok_rows, local_heads * GROUP * HS)
    partial_value = jnp.einsum(
        "tj,dj->td", mixed_flat, full_out.reshape(width, -1), preferred_element_type=jnp.float32
    )
    summed = lax.psum_scatter(
        partial_value.astype(jnp.bfloat16), "row", scatter_dimension=1, tiled=True
    ).astype(jnp.float32)
    col_width = width // row_count
    packed_cols = lax.dynamic_slice_in_dim(packed_f, row_index * col_width, col_width, 1)
    total = packed_cols + summed
    hidden_out = total.astype(jnp.bfloat16)
    score_cols = lax.dynamic_slice_in_dim(score_weights, row_index * col_width, col_width, 0)
    token_scores = jnp.dot(total, score_cols, precision=lax.Precision.HIGHEST)
    record_part = jnp.dot(
        token_scores, matches.astype(jnp.float32), precision=lax.Precision.HIGHEST
    )
    record_total = lax.psum(record_part, "row")
    record_scores = (record_total / record_lens.astype(jnp.float32))[None, :]
    return (hidden_out, record_scores)


def solution(mesh):
    in_specs = (
        P("row", None, "reader", None),
        P(),
        P(),
        P(),
        P(),
        P("reader", "row", None),
        P("reader", "row", None),
        P(),
    )
    out_specs = (P("reader", "row"), P("reader", None))
    return jax.shard_map(
        on_device, mesh=mesh, in_specs=in_specs, out_specs=out_specs, check_vma=False
    )
```

profile of v0, /device:TPU:1, one launch (start us, length us, event | category | flops | bytes accessed | tf_op | source)
XLA Modules:
  0.0 561.5 jit_solution(11207179706539714900)
XLA Ops:
  7.2 0.0 copy-start
  7.2 0.0 copy-start.4
  7.2 0.0 copy-start.2
  7.2 0.0 all-gather.4.cloned.1.call-start
  7.3 0.8 dynamic-slice_bitcast_fusion
  8.1 0.6 iota_reduce_fusion
  8.7 0.0 copy-done
  8.8 2.0 gather_fusion
  10.8 36.0 %all_to_all.5 = bf16[32,8,4096]{2,1,0:T(8,128)(2,1)} all-to-all(bf16[32,8,4096]{2,1,0:T(8,128)(2,1)} %gather_fusion), channel_id=1, replica_groups=mesh['row'=4,'reader'=32] {'reader'}, dimensions={0} | all-to-all | bytes 4194304 | tf_op jit(solution)/shard_map/all_to_all | solution.py:56
  46.8 0.0 all-gather.4.cloned.1.call-update
  46.8 0.0 all-gather.6.cloned.1.call-start
  46.9 0.7 all-gather.6.cloned.1.call-update
  47.6 0.0 all-gather.8.cloned.1.call-start
  47.6 0.7 all-gather.8.cloned.1.call-update
  48.3 0.0 reduce-scatter.2.cloned.1.call-start
  48.4 0.6 iota_reduce_fusion.1
  49.1 0.6 gather_fusion.3
  49.7 0.2 reduce-window.4
  49.9 0.1 convert_reduce_fusion
  50.0 0.1 select_reduce_fusion
  50.1 0.1 fusion.55
  50.2 0.0 copy-done.3
  50.2 9.0 %gather_fusion.2 = s32[896]{0:T(1024)S(1)} fusion(s32[4,32,256]{2,1,0:T(8,128)S(1)} %copy-done.3, s32[896]{0:T(1024)S(1)} %get-tuple-element.6), kind=kCustom, calls=%fused_computation.2 | custom fusion | bytes 17920 | tf_op jit(solution)/shard_map/gather | solution.py:51
  59.2 0.9 multiply_cosine_fusion
  60.1 1.2 fusion.15
  61.3 48.4 %all-gather.4.cloned.1.call-done = bf16[4,256,4096]{2,1,0:T(8,128)(2,1)} async-done(((bf16[1,256,4096]{2,1,0:T(8,128)(2,1)}), bf16[4,256,4096]{2,1,0:T(8,128)(2,1)}) %all-gather.4.cloned.1.call-update) | async-done | bytes 8388624 | tf_op jit(solution)/shard_map/all_gather | solution.py:58
  109.7 19.4 %gather_fusion.1 = bf16[896,4096]{1,0:T(8,128)(2,1)} fusion(bf16[1024,4096]{1,0:T(8,128)(2,1)} %bitcast.91, s32[1024]{0:T(1024)S(1)} %pad_clamp_fusion), kind=kCustom, calls=%fused_computation.1 | custom fusion | bytes 14683648 | tf_op jit(solution)/shard_map/gather | solution.py:59
  129.2 4.6 multiply_reduce_fusion
  133.8 130.7 %all-gather.6.cloned.1.call-done = bf16[4096,1,1280]{2,0,1:T(8,128)(2,1)} async-done(((bf16[128,1,1280]{2,0,1:T(8,128)(2,1)}), bf16[4096,1,1280]{2,0,1:T(8,128)(2,1)}) %all-gather.6.cloned.1.call-update) | async-done | bytes 10485776 | tf_op jit(solution)/shard_map/all_gather | solution.py:64
  264.6 14.3 %copy.22 = bf16[1280,4096]{1,0:T(8,128)(2,1)} copy(bf16[1280,4096]{0,1:T(8,128)(2,1)} %bitcast.92) | data formatting | bytes 20971520 | tf_op jit(solution)/shard_map/dot_general | solution.py:67
  278.9 15.1 %fusion.18 = f32[896,1,10,128]{0,3,2,1:T(8,128)S(1)} fusion(bf16[10,128,4096]{2,1,0:T(8,128)(2,1)} %bitcast.93, f32[4096]{0:T(1024)S(1)} %copy-done.5, f32[896]{0:T(1024)S(1)} %add_rsqrt_fusion, bf16[896,4096]{1,0:T(8,128)(2,1)} %gather_fusion.1), kind=kOutput, calls=%fused_computation.26 | convolution fusion | flops 9409921024 | bytes 22433280 | tf_op jit(solution)/shard_map/dot_general | solution.py:67
  294.0 0.9 fusion.44
  294.9 0.5 fusion.29
  295.5 11.1 %fusion = (f32[8,896]{1,0:T(8,128)S(1)}, f32[896,896,8]{1,0,2:T(8,128)}) fusion(pred[896,896]{0,1:T(8,128)(4,1)S(1)} %fusion.15, bf16[896,8,64]{0,2,1:T(8,128)(2,1)S(1)} %get-tuple-element.11, bf16[896,8,64]{0,2,1:T(8,128)(2,1)S(1)} %get-tuple-element.10, bf16[896,64]{0,1:T(8,128)(2,1)S(1)} %get-tuple-element.13, bf16[896,64]{0,1:T(8,128)(2,1)S(1)} %get-tuple-element.12), kind=kOutput, calls=%fused_computation.7 | convolution fusion | flops 1667556352 | bytes 28585984 | tf_op jit(solution)/shard_map/qhgd,khd->hgqk/dot_general | solution.py:81
  306.6 12.1 %fusion.1 = f32[8,896]{1,0:T(8,128)S(1)} fusion(f32[896,896,8]{1,0,2:T(8,128)} %get-tuple-element.17, f32[8,896]{1,0:T(8,128)S(1)} %get-tuple-element.16, pred[896,896]{0,1:T(8,128)(4,1)S(1)} %fusion.15), kind=kLoop, calls=%fused_computation.8 | loop fusion | flops 32105472 | bytes 26550272 | tf_op jit(solution)/shard_map/reduce_sum | solution.py:29
  318.6 14.9 %fusion.25 = bf16[128,8,896]{2,0,1:T(8,128)(2,1)} fusion(f32[8,896]{1,0:T(8,128)S(1)} %fusion.1, f32[8,896]{1,0:T(8,128)S(1)} %get-tuple-element.16, f32[896,896,8]{1,0,2:T(8,128)} %get-tuple-element.17, pred[896,896]{0,1:T(8,128)(4,1)S(1)} %fusion.15, f32[896,1,10,128]{0,3,2,1:T(8,128)S(1)} %fusion.18), kind=kOutput, calls=%fused_computation.33 | convolution fusion | flops 1683619840 | bytes 28614656 | tf_op jit(solution)/shard_map/hgqk,khd->qhgd/dot_general | solution.py:85
  333.5 97.7 %all-gather.8.cloned.1.call-done = bf16[4096,1,1024]{2,0,1:T(8,128)(2,1)} async-done(((bf16[128,1,1024]{2,0,1:T(8,128)(2,1)}), bf16[4096,1,1024]{2,0,1:T(8,128)(2,1)}) %all-gather.8.cloned.1.call-update) | async-done | bytes 8388624 | tf_op jit(solution)/shard_map/all_gather | solution.py:65
  431.2 12.6 %fusion.12 = bf16[896,4096]{1,0:T(8,128)(2,1)} fusion(bf16[896,1024]{0,1:T(8,128)(2,1)} %bitcast.96, bf16[4096,1,1024]{2,0,1:T(8,128)(2,1)} %all-gather.8.cloned.1.call-done), kind=kOutput, calls=%fused_computation.20 | convolution fusion | flops 7519862784 | bytes 17563648 | tf_op jit(solution)/shard_map/tj,dj->td/dot_general | solution.py:89
  443.8 0.0 reduce-scatter.2.cloned.1.call-update
  443.9 0.0 dynamic-slice-start
  443.9 0.0 copy-start.1
  443.9 10.4 %convert_element_type.57 = f32[896,4096]{1,0:T(8,128)} convert(bf16[896,4096]{1,0:T(8,128)(2,1)} %gather_fusion.1) | non-fusion elementwise | flops 3670016 | bytes 22020096 | tf_op jit(solution)/shard_map/convert_element_type | solution.py:60
  454.3 82.3 %reduce-scatter.2.cloned.1.call-done = bf16[896,1024]{1,0:T(8,128)(2,1)} async-done(((bf16[896,4096]{1,0:T(8,128)(2,1)}), bf16[896,1024]{1,0:T(8,128)(2,1)}) %reduce-scatter.2.cloned.1.call-update) | async-done | bytes 1835024 | tf_op jit(solution)/shard_map/reduce_scatter | solution.py:92
  536.7 5.9 %fusion.28 = f32[896,1]{0,1:T(1,128)S(1)} fusion(f32[1024,1]{0,1:T(1,128)S(1)} %bitcast.95, bf16[896,1024]{1,0:T(8,128)(2,1)} %reduce-scatter.2.cloned.1.call-done, f32[896,4096]{1,0:T(8,128)} %convert_element_type.57, s32[]{:T(128)} %select_n.96), kind=kOutput, calls=%fused_computation.34 | convolution fusion | flops 12845056 | bytes 5513216 | tf_op jit(solution)/shard_map/dot_general | solution.py:100
  542.6 0.1 convolution_bitcast_fusion
  542.7 7.2 %psum.7 = f32[4]{0:T(128)S(1)} all-reduce(f32[4]{0:T(128)S(1)} %convolution_bitcast_fusion), channel_id=1, replica_groups=mesh['row'=4,'reader'=32] {'row'}, use_global_device_ids=true, to_apply=%region_10.11 | all-reduce | flops 4 | bytes 32 | tf_op jit(solution)/shard_map/psum | solution.py:104
  549.9 0.5 fusion.57
  550.4 4.5 fusion.17
  (21 shorter events, 0.1 us)
Async XLA Ops:
  7.2 1.6 copy-start
  7.2 41.2 %copy-start.4 = (s32[4,32]{1,0:T(4,128)S(1)}, s32[4,32]{1,0:T(4,128)}, u32[]{:S(2)}) copy-start(s32[4,32]{1,0:T(4,128)} %param.10) | copy-start | bytes 1540
  7.2 41.9 %copy-start.2 = (s32[4,32]{1,0:T(4,128)S(1)}, s32[4,32]{1,0:T(4,128)}, u32[]{:S(2)}) copy-start(s32[4,32]{1,0:T(4,128)} %param.9) | copy-start | bytes 1540
  7.2 43.0 %copy-start.3 = (s32[4,32,256]{2,1,0:T(8,128)S(1)}, s32[4,32,256]{2,1,0:T(8,128)}, u32[]{:S(2)}) copy-start(s32[4,32,256]{2,1,0:T(8,128)} %param.11) | copy-start | bytes 393220
  7.2 102.5 %all-gather.4.cloned.1.call-start = ((), (), s32[]{:S(2)}) async-start(), calls=%async_computation.2 | async-start | bytes 10485760 | tf_op jit(solution)/shard_map/all_gather | solution.py:58
  46.8 217.7 %all-gather.6.cloned.1.call-start = ((), (), s32[]{:S(2)}) async-start(), calls=%async_computation.3 | async-start | bytes 10813440 | tf_op jit(solution)/shard_map/all_gather | solution.py:64
  47.6 383.6 %all-gather.8.cloned.1.call-start = ((), (), s32[]{:S(2)}) async-start(), calls=%async_computation.4 | async-start | bytes 8650752 | tf_op jit(solution)/shard_map/all_gather | solution.py:65
  48.3 488.3 %reduce-scatter.2.cloned.1.call-start = ((), (), s32[]{:S(2)}) async-start(), calls=%async_computation.5 | async-start | bytes 9175040 | tf_op jit(solution)/shard_map/reduce_scatter | solution.py:92
  264.6 14.3 %copy-start.5 = (f32[4096]{0:T(1024)S(1)}, f32[4096]{0:T(1024)}, u32[]{:S(2)}) copy-start(f32[4096]{0:T(1024)} %param.12) | copy-start | bytes 49156
  443.9 92.8 %dynamic-slice-start = ((f32[4096]{0:T(1024)}, s32[]{:T(128)}), f32[1024]{0:T(1024)S(1)}, s32[]{:S(2)}) async-start(f32[4096]{0:T(1024)} %param.15, s32[]{:T(128)} %select_n.96), calls=%async_computation.6 | async-start | bytes 8704 | tf_op jit(solution)/shard_map/dynamic_slice | solution.py:99
  443.9 111.0 %copy-start.1 = (bf16[1,32,8,4096]{3,2,1,0:T(8,128)(2,1)S(1)}, bf16[1,32,8,4096]{3,2,1,0:T(8,128)(2,1)}, u32[]{:S(2)}) copy-start(bf16[1,32,8,4096]{3,2,1,0:T(8,128)(2,1)} %param.8) | copy-start | bytes 6291460
Sparse Core Ops, SparseCore 0:
  47.0 62.7 all-gather.3
  111.4 153.1 all-gather.5
  266.2 164.9 all-gather.7
  444.0 92.6 reduce-scatter.1
where the time goes:
time: 562 us; the launch traced here: 561 us
  waiting for transfers between devices  361 us (64%)
  matrix products  59.7 us (11%)
  local copies, waits for them, and re-layouts  46.4 us (8%)
  blocking collectives  43.2 us (8%)
  other arithmetic  37.4 us (7%)
  between operations  14 us (2%)
    all_gather x1, waiting for transfers between devices, on_device(): lax.all_gather(w_qkv, 'reader', axis=0, tiled=True)  131 us
    all_gather x1, waiting for transfers between devices, on_device(): lax.all_gather(w_out, 'reader', axis=0, tiled=True)  97.7 us
    reduce_scatter x1, waiting for transfers between devices, on_device(): lax.psum_scatter(partial_value.astype(jnp.bfloat16), 'row', scatter_dimen...  82.3 us
    all_gather x1, waiting for transfers between devices, on_device(): gathered = lax.all_gather(own_record, 'row', axis=0, tiled=True)  48.4 us
    all_to_all x1, blocking collectives, on_device(): lax.all_to_all(send_block, 'reader', split_axis=0, concat_axis=0, tiled=T...  36 us
    gather x1, local copies, waits for them, and re-layouts, on_device(): gathered.reshape(row_count * RECLEN, width)[owner * RECLEN + within]  19.4 us
    dot_general x1, matrix products, on_device(): jnp.dot(normed, full_qkv.reshape(width, -1), preferred_element_type=jnp.f...  15.1 us
    dot_general x1, matrix products, on_device(): jnp.einsum('hgqk,khd->qhgd', probs, values, preferred_element_type=jnp.fl...  14.9 us
  transfers between devices with their start and end apart: 4, of which 4 were waited for; matrix products, arithmetic and copies ran while one was open for 21% of the time, Pallas kernels for 0%

commit v1 on v0

--- a/solution.py
+++ b/solution.py
@@ -55,7 +55,8 @@
     send_block = records[0][outgoing]
     arrived = lax.all_to_all(send_block, "reader", split_axis=0, concat_axis=0, tiled=True)
     own_record = arrived.reshape(1, reader_count * slot_count, width)
-    gathered = lax.all_gather(own_record, "row", axis=0, tiled=True)
+    sent = jnp.stack([own_record] * lax.axis_size("row"))
+    gathered = jnp.concatenate(lax.all_to_all(sent, "row", 0, 0), axis=0)
     packed = gathered.reshape(row_count * RECLEN, width)[owner * RECLEN + within]
     packed_f = packed.astype(jnp.float32)
     scale = lax.rsqrt(jnp.mean(packed_f * packed_f, axis=1, keepdims=True) + 1e-05)

time: 562 us -> 529 us (0.941)
  waiting for transfers between devices: 361 us -> 304 us
  blocking collectives: 43.2 us -> 55.6 us
  starting transfers between devices: 0.16 us -> 6.98 us
    all_to_all x0 -> x1, waiting for transfers between devices: none -> 167 us  [on_device(): gathered = jnp.concatenate(lax.all_to_all(sent, 'row', 0, 0), axis=0)]
    all_gather x1, waiting for transfers between devices: 131 us -> 0.02 us  [on_device(): lax.all_gather(w_qkv, 'reader', axis=0, tiled=True)]
    all_gather x1 -> x0, waiting for transfers between devices: 48.4 us -> none  [on_device(): gathered = lax.all_gather(own_record, 'row', axis=0, tiled=True)]
    all_gather x1, waiting for transfers between devices: 97.7 us -> 53.3 us  [on_device(): lax.all_gather(w_out, 'reader', axis=0, tiled=True)]
    all_to_all x1, blocking collectives: 36 us -> 48.4 us  [on_device(): lax.all_to_all(send_block, 'reader', split_axis=0, concat_axis=0, tiled=T...]
    all_to_all x0 -> x1, starting transfers between devices: none -> 6.9 us  [on_device(): gathered = jnp.concatenate(lax.all_to_all(sent, 'row', 0, 0), axis=0)]
  transfers between devices with their start and end apart: 4 -> 4, of which waited for: 4 -> 3; matrix products, arithmetic and copies ran while one was open for 21% -> 23% of each run, Pallas kernels for 0% -> 0%
where the time goes in v1:
time: 529 us; the launch traced here: 528 us
  waiting for transfers between devices  304 us (57%)
  matrix products  59.8 us (11%)
  blocking collectives  55.6 us (11%)
  local copies, waits for them, and re-layouts  50.5 us (10%)
  other arithmetic  37.4 us (7%)
  between operations  13.9 us (3%)
  starting transfers between devices  6.98 us (1%)
    all_to_all x1, waiting for transfers between devices, on_device(): gathered = jnp.concatenate(lax.all_to_all(sent, 'row', 0, 0), axis=0)  167 us
    reduce_scatter x1, waiting for transfers between devices, on_device(): lax.psum_scatter(partial_value.astype(jnp.bfloat16), 'row', scatter_dimen...  82.2 us
    all_gather x1, waiting for transfers between devices, on_device(): lax.all_gather(w_out, 'reader', axis=0, tiled=True)  53.3 us
    all_to_all x1, blocking collectives, on_device(): lax.all_to_all(send_block, 'reader', split_axis=0, concat_axis=0, tiled=T...  48.4 us
    gather x1, local copies, waits for them, and re-layouts, on_device(): gathered.reshape(row_count * RECLEN, width)[owner * RECLEN + within]  19.4 us
    dot_general x1, matrix products, on_device(): jnp.dot(normed, full_qkv.reshape(width, -1), preferred_element_type=jnp.f...  15.2 us
    dot_general x1, matrix products, on_device(): jnp.einsum('hgqk,khd->qhgd', probs, values, preferred_element_type=jnp.fl...  14.9 us
    dot_general x1, local copies, waits for them, and re-layouts, on_device(): jnp.dot(normed, full_qkv.reshape(width, -1), preferred_element_type=jnp.f...  14.3 us
  transfers between devices with their start and end apart: 4, of which 3 were waited for; matrix products, arithmetic and copies ran while one was open for 23% of the time, Pallas kernels for 0%

profile of v1, /device:TPU:1, one launch (start us, length us, event | category | flops | bytes accessed | tf_op | source)
XLA Modules:
  0.0 528.1 jit_solution(9527262755189528749)
XLA Ops:
  7.2 0.0 copy-start
  7.2 0.0 all-gather.3.cloned.1.call-start
  7.2 0.7 all-gather.3.cloned.1.call-update
  7.9 0.7 dynamic-slice_bitcast_fusion
  8.6 0.6 iota_reduce_fusion
  9.3 0.0 copy-done
  9.3 2.0 gather_fusion
  11.2 48.4 %all_to_all.10 = bf16[32,8,4096]{2,1,0:T(8,128)(2,1)S(1)} all-to-all(bf16[32,8,4096]{2,1,0:T(8,128)(2,1)} %gather_fusion), channel_id=1, replica_groups=mesh['row'=4,'reader'=32] {'reader'}, dimensions={0} | all-to-all | bytes 4194304 | tf_op jit(solution)/shard_map/all_to_all | solution.py:56
  59.7 4.3 stack.3
  64.0 6.9 %all-to-all-start.1 = ((bf16[4,1,256,4096]{3,2,1,0:T(8,128)(2,1)}), bf16[4,1,256,4096]{3,2,1,0:T(8,128)(2,1)}, u32[]{:S(2)}, u32[]{:S(2)}) async-start(bf16[4,1,256,4096]{3,2,1,0:T(8,128)(2,1)} %stack.3), calls=%async_computation.1 | async-start | bytes 16777216 | tf_op jit(solution)/shard_map/all_to_all | solution.py:59
  70.9 0.0 all-gather.5.cloned.1.call-start
  70.9 0.7 all-gather.5.cloned.1.call-update
  71.6 0.0 reduce-scatter.2.cloned.1.call-start
  71.7 0.6 iota_reduce_fusion.1
  72.4 0.0 copy-done.2
  72.4 0.6 gather_fusion.3
  73.0 0.2 reduce-window.4
  73.2 0.1 convert_reduce_fusion
  73.3 0.1 select_reduce_fusion
  73.4 0.1 fusion.55
  73.5 9.0 %gather_fusion.2 = s32[896]{0:T(1024)S(1)} fusion(s32[4,32,256]{2,1,0:T(8,128)S(1)} %copy-done.3, s32[896]{0:T(1024)S(1)} %get-tuple-element.6), kind=kCustom, calls=%fused_computation.2 | custom fusion | bytes 17920 | tf_op jit(solution)/shard_map/gather | solution.py:51
  82.5 0.9 multiply_cosine_fusion
  83.4 1.2 fusion.15
  84.6 166.9 %all-to-all-done.1 = bf16[4,1,256,4096]{3,2,1,0:T(8,128)(2,1)} async-done(((bf16[4,1,256,4096]{3,2,1,0:T(8,128)(2,1)}), bf16[4,1,256,4096]{3,2,1,0:T(8,128)(2,1)}, u32[]{:S(2)}, u32[]{:S(2)}) %all-to-all-start.1) | async-done | bytes 8388640 | tf_op jit(solution)/shard_map/all_to_all | solution.py:59
  251.6 19.4 %gather_fusion.1 = bf16[896,4096]{1,0:T(8,128)(2,1)} fusion(bf16[1024,4096]{1,0:T(8,128)(2,1)} %bitcast.3, s32[1024]{0:T(1024)S(1)} %pad_clamp_fusion), kind=kCustom, calls=%fused_computation.1 | custom fusion | bytes 14683648 | tf_op jit(solution)/shard_map/gather | solution.py:60
  271.0 4.6 multiply_reduce_fusion
  275.6 0.0 all-gather.3.cloned.1.call-done
  275.7 0.0 copy-start.5
  275.7 14.3 %copy.22 = bf16[1280,4096]{1,0:T(8,128)(2,1)} copy(bf16[1280,4096]{0,1:T(8,128)(2,1)} %bitcast.91) | data formatting | bytes 20971520 | tf_op jit(solution)/shard_map/dot_general | solution.py:68
  290.0 0.0 copy-done.5
  290.0 15.2 %fusion.18 = f32[896,1,10,128]{0,3,2,1:T(8,128)S(1)} fusion(bf16[10,128,4096]{2,1,0:T(8,128)(2,1)} %bitcast.92, f32[4096]{0:T(1024)S(1)} %copy-done.5, f32[896]{0:T(1024)S(1)} %add_rsqrt_fusion, bf16[896,4096]{1,0:T(8,128)(2,1)} %gather_fusion.1), kind=kOutput, calls=%fused_computation.26 | convolution fusion | flops 9409921024 | bytes 22433280 | tf_op jit(solution)/shard_map/dot_general | solution.py:68
  305.2 0.9 fusion.44
  306.1 0.5 fusion.29
  306.7 11.1 %fusion = (f32[8,896]{1,0:T(8,128)S(1)}, f32[896,896,8]{1,0,2:T(8,128)}) fusion(pred[896,896]{0,1:T(8,128)(4,1)S(1)} %fusion.15, bf16[896,8,64]{0,2,1:T(8,128)(2,1)S(1)} %get-tuple-element.11, bf16[896,8,64]{0,2,1:T(8,128)(2,1)S(1)} %get-tuple-element.10, bf16[896,64]{0,1:T(8,128)(2,1)S(1)} %get-tuple-element.13, bf16[896,64]{0,1:T(8,128)(2,1)S(1)} %get-tuple-element.12), kind=kOutput, calls=%fused_computation.7 | convolution fusion | flops 1667556352 | bytes 28585984 | tf_op jit(solution)/shard_map/qhgd,khd->hgqk/dot_general | solution.py:82
  317.8 12.1 %fusion.1 = f32[8,896]{1,0:T(8,128)S(1)} fusion(f32[896,896,8]{1,0,2:T(8,128)} %get-tuple-element.17, f32[8,896]{1,0:T(8,128)S(1)} %get-tuple-element.16, pred[896,896]{0,1:T(8,128)(4,1)S(1)} %fusion.15), kind=kLoop, calls=%fused_computation.8 | loop fusion | flops 32105472 | bytes 26550272 | tf_op jit(solution)/shard_map/reduce_sum | solution.py:29
  329.9 14.9 %fusion.25 = bf16[128,8,896]{2,0,1:T(8,128)(2,1)} fusion(f32[8,896]{1,0:T(8,128)S(1)} %fusion.1, f32[8,896]{1,0:T(8,128)S(1)} %get-tuple-element.16, f32[896,896,8]{1,0,2:T(8,128)} %get-tuple-element.17, pred[896,896]{0,1:T(8,128)(4,1)S(1)} %fusion.15, f32[896,1,10,128]{0,3,2,1:T(8,128)S(1)} %fusion.18), kind=kOutput, calls=%fused_computation.33 | convolution fusion | flops 1683619840 | bytes 28614656 | tf_op jit(solution)/shard_map/hgqk,khd->qhgd/dot_general | solution.py:86
  344.7 53.3 %all-gather.5.cloned.1.call-done = bf16[4096,1,1024]{2,0,1:T(8,128)(2,1)} async-done(((bf16[128,1,1024]{2,0,1:T(8,128)(2,1)}), bf16[4096,1,1024]{2,0,1:T(8,128)(2,1)}) %all-gather.5.cloned.1.call-update) | async-done | bytes 8388624 | tf_op jit(solution)/shard_map/all_gather | solution.py:66
  398.0 12.6 %fusion.12 = bf16[896,4096]{1,0:T(8,128)(2,1)} fusion(bf16[896,1024]{0,1:T(8,128)(2,1)} %bitcast.95, bf16[4096,1,1024]{2,0,1:T(8,128)(2,1)} %all-gather.5.cloned.1.call-done), kind=kOutput, calls=%fused_computation.20 | convolution fusion | flops 7519862784 | bytes 17563648 | tf_op jit(solution)/shard_map/tj,dj->td/dot_general | solution.py:90
  410.6 0.0 reduce-scatter.2.cloned.1.call-update
  410.7 0.0 dynamic-slice-start
  410.7 0.0 copy-start.1
  410.7 10.4 %convert_element_type.57 = f32[896,4096]{1,0:T(8,128)} convert(bf16[896,4096]{1,0:T(8,128)(2,1)} %gather_fusion.1) | non-fusion elementwise | flops 3670016 | bytes 22020096 | tf_op jit(solution)/shard_map/convert_element_type | solution.py:61
  421.1 82.2 %reduce-scatter.2.cloned.1.call-done = bf16[896,1024]{1,0:T(8,128)(2,1)} async-done(((bf16[896,4096]{1,0:T(8,128)(2,1)}), bf16[896,1024]{1,0:T(8,128)(2,1)}) %reduce-scatter.2.cloned.1.call-update) | async-done | bytes 1835024 | tf_op jit(solution)/shard_map/reduce_scatter | solution.py:93
  503.3 5.9 %fusion.28 = f32[896,1]{0,1:T(1,128)S(1)} fusion(f32[1024,1]{0,1:T(1,128)S(1)} %bitcast.94, bf16[896,1024]{1,0:T(8,128)(2,1)} %reduce-scatter.2.cloned.1.call-done, f32[896,4096]{1,0:T(8,128)} %convert_element_type.57, s32[]{:T(128)} %select_n.96), kind=kOutput, calls=%fused_computation.34 | convolution fusion | flops 12845056 | bytes 5513216 | tf_op jit(solution)/shard_map/dot_general | solution.py:101
  509.2 0.1 convolution_bitcast_fusion
  509.3 7.2 %psum.7 = f32[4]{0:T(128)S(1)} all-reduce(f32[4]{0:T(128)S(1)} %convolution_bitcast_fusion), channel_id=1, replica_groups=mesh['row'=4,'reader'=32] {'row'}, use_global_device_ids=true, to_apply=%region_10.11 | all-reduce | flops 4 | bytes 32 | tf_op jit(solution)/shard_map/psum | solution.py:105
  516.5 0.5 fusion.57
  517.1 4.5 fusion.17
  (21 shorter events, 0.1 us)
Async XLA Ops:
  7.2 2.1 copy-start
  7.2 268.5 %all-gather.3.cloned.1.call-start = ((), (), s32[]{:S(2)}) async-start(), calls=%async_computation.3 | async-start | bytes 10813440 | tf_op jit(solution)/shard_map/all_gather | solution.py:65
  64.0 7.7 %copy-start.4 = (s32[4,32]{1,0:T(4,128)S(1)}, s32[4,32]{1,0:T(4,128)}, u32[]{:S(2)}) copy-start(s32[4,32]{1,0:T(4,128)} %param.10) | copy-start | bytes 1540
  64.0 8.4 %copy-start.2 = (s32[4,32]{1,0:T(4,128)S(1)}, s32[4,32]{1,0:T(4,128)}, u32[]{:S(2)}) copy-start(s32[4,32]{1,0:T(4,128)} %param.9) | copy-start | bytes 1540
  64.0 9.5 %copy-start.3 = (s32[4,32,256]{2,1,0:T(8,128)S(1)}, s32[4,32,256]{2,1,0:T(8,128)}, u32[]{:S(2)}) copy-start(s32[4,32,256]{2,1,0:T(8,128)} %param.11) | copy-start | bytes 393220
  64.0 187.6 %all-to-all-start.1 = ((bf16[4,1,256,4096]{3,2,1,0:T(8,128)(2,1)}), bf16[4,1,256,4096]{3,2,1,0:T(8,128)(2,1)}, u32[]{:S(2)}, u32[]{:S(2)}) async-start(bf16[4,1,256,4096]{3,2,1,0:T(8,128)(2,1)} %stack.3), calls=%async_computation.1 | async-start | bytes 16777216 | tf_op jit(solution)/shard_map/all_to_all | solution.py:59
  70.9 327.1 %all-gather.5.cloned.1.call-start = ((), (), s32[]{:S(2)}) async-start(), calls=%async_computation.4 | async-start | bytes 8650752 | tf_op jit(solution)/shard_map/all_gather | solution.py:66
  71.6 431.7 %reduce-scatter.2.cloned.1.call-start = ((), (), s32[]{:S(2)}) async-start(), calls=%async_computation.5 | async-start | bytes 9175040 | tf_op jit(solution)/shard_map/reduce_scatter | solution.py:93
  275.7 14.3 %copy-start.5 = (f32[4096]{0:T(1024)S(1)}, f32[4096]{0:T(1024)}, u32[]{:S(2)}) copy-start(f32[4096]{0:T(1024)} %param.12) | copy-start | bytes 49156
  410.7 92.6 %dynamic-slice-start = ((f32[4096]{0:T(1024)}, s32[]{:T(128)}), f32[1024]{0:T(1024)S(1)}, s32[]{:S(2)}) async-start(f32[4096]{0:T(1024)} %param.15, s32[]{:T(128)} %select_n.96), calls=%async_computation.6 | async-start | bytes 8704 | tf_op jit(solution)/shard_map/dynamic_slice | solution.py:100
  410.7 110.9 %copy-start.1 = (bf16[1,32,8,4096]{3,2,1,0:T(8,128)(2,1)S(1)}, bf16[1,32,8,4096]{3,2,1,0:T(8,128)(2,1)}, u32[]{:S(2)}) copy-start(bf16[1,32,8,4096]{3,2,1,0:T(8,128)(2,1)} %param.8) | copy-start | bytes 6291460
Sparse Core Ops, SparseCore 0:
  9.7 238.1 all-gather.2
  249.5 148.4 all-gather.4
  410.8 92.4 reduce-scatter.1
